TPU v7x, 512 devices: a whole 4x8x8 slice. The times are simulated.
512 devices in a mesh: row: 16 (over y, core), col: 8 (over z), depth: 4 (over x).
Axes of the slice: x: 4, y: 8, z: 8, core: 2. Of those that a mesh axis runs over, the one named last changes fastest.
Arguments:
- density: float32 [512, 5, 128, 128], P(('row', 'depth'), None, 'col'), may hold values from -0.6 to 0.6
- pattern: int32 [512, 5], P(('row', 'depth')), may hold values 0 or 1
Outputs:
- purified: float32 [512, 5, 128, 128], P(('row', 'depth'), None, 'col')
All inputs are finite; a program needn't handle non-finite values. No bound on the sum of `pattern` on one device may be relied on, other than what follows from the above.
Results may differ from a plain program's by a relative error of at most 0.0001.
Values sent between devices are 32-bit elements; how exact they have to be, the bound alone decides.
No kernel may reach another device: no remote copies, remote signals or barrier semaphores. Data moves between devices by JAX's collectives and lax.ppermute only.
A program may use at most 64 MiB of HBM per device.

v0:
```python
import jax
import jax.numpy as jnp
from jax import lax
from jax.sharding import PartitionSpec as P

HALF = 2
WIDE = 5


def with_halo(cells, sides, width):
    for axis, dim in sides:
        count = lax.axis_size(axis)
        head = lax.slice_in_dim(cells, 0, width, axis=dim)
        tail = lax.slice_in_dim(cells, cells.shape[dim] - width, cells.shape[dim], axis=dim)
        cells = jnp.concatenate(
            [
                lax.ppermute(tail, axis, [(i, (i + 1) % count) for i in range(count)]),
                cells,
                lax.ppermute(head, axis, [((i + 1) % count, i) for i in range(count)]),
            ],
            axis=dim,
        )
    return cells


def banded_local(left_tiles, extended, pattern):
    rows_here = left_tiles.shape[0]
    summed = jnp.zeros(left_tiles.shape, jnp.float32)
    for source in range(WIDE):
        first_slot = max(0, source - HALF)
        last_slot = min(WIDE, source + HALF + 1)
        partner = extended[
            source : source + rows_here, first_slot - source + HALF : last_slot - source + HALF
        ]
        contrib = jnp.einsum(
            "iab,itbc->itac", left_tiles[:, source], partner, precision=lax.Precision.HIGHEST
        )
        summed = summed.at[:, first_slot:last_slot].add(contrib)
    return summed * pattern[:, :, None, None].astype(jnp.float32)


def shards(density, pattern):
    masked = density * pattern[:, :, None, None].astype(jnp.float32)
    whole_tiles = lax.all_gather(masked, "col", axis=2, tiled=True)
    extended = with_halo(whole_tiles, ((("row", "depth"), 0),), HALF)
    square = banded_local(masked, extended, pattern)
    cube = banded_local(square, extended, pattern)
    return 3.0 * square - 2.0 * cube


def solution(mesh):
    in_specs = (P(("row", "depth"), None, "col", None), P(("row", "depth"), None))
    out_specs = P(("row", "depth"), None, "col", None)
    return jax.shard_map(shards, mesh=mesh, in_specs=in_specs, out_specs=out_specs, check_vma=False)
```

profile of v0, /device:TPU:1, one launch (start us, length us, event | category | flops | bytes accessed | tf_op | source)
XLA Modules:
  0.0 108.2 jit_solution(13460640927756689920)
XLA Ops:
  6.5 0.0 all-gather.2.cloned.1.call-start
  6.5 0.7 convert_element_type.6
  7.2 0.1 copy.3
  7.3 1.8 %copy_multiply_fusion = f32[8,5,16,128]{3,2,0,1:T(8,128)} fusion(f32[8,5,16,128]{3,2,1,0:T(8,128)} %param.26, f32[8,5]{0,1:T(8,128)S(1)} %copy.3), kind=kLoop, calls=%fused_computation.18 | loop fusion | flops 81920 | bytes 655520 | tf_op jit(solution)/shard_map/mul | solution.py:43
  9.1 0.0 all-gather.2.cloned.1.call-update
  9.1 48.3 %all-gather.2.cloned.1.call-done = f32[8,5,128,128]{3,2,0,1:T(8,128)} async-done(((f32[8,5,16,128]{3,2,0,1:T(8,128)}), f32[8,5,128,128]{3,2,0,1:T(8,128)}) %all-gather.2.cloned.1.call-update) | async-done | bytes 2621456 | tf_op jit(solution)/shard_map/all_gather | solution.py:44
  57.5 0.0 copy-start
  57.5 1.5 %fusion.10 = (f32[2,5,128,128]{3,2,0,1:T(8,128)S(1)}, f32[2,5,128,128]{3,2,0,1:T(8,128)S(1)}) fusion(f32[8,5,128,128]{3,2,0,1:T(8,128)} %all-gather.2.cloned.1.call-done), kind=kLoop, calls=%fused_computation.41 | loop fusion | bytes 2621440 | tf_op jit(solution)/shard_map/slice | solution.py:13
  59.0 3.1 %collective-permute-start = (f32[2,5,128,128]{3,2,0,1:T(8,128)S(1)}, f32[2,5,128,128]{3,2,0,1:T(8,128)S(1)}, u32[]{:S(2)}, u32[]{:S(2)}) collective-permute-start(f32[2,5,128,128]{3,2,0,1:T(8,128)S(1)} %get-tuple-element.142), channel_id=1, source_target_pairs={{0,1},{1,2},{2,3},{3,32},{32,33},{33,34},{34,35},{35,64},{64,65},{... | collective-permute-start | bytes 1966088 | tf_op jit(solution)/shard_map/ppermute | solution.py:17
  62.1 6.9 %collective-permute-start.1 = (f32[2,5,128,128]{3,2,0,1:T(8,128)S(1)}, f32[2,5,128,128]{3,2,0,1:T(8,128)S(1)}, u32[]{:S(2)}, u32[]{:S(2)}) collective-permute-start(f32[2,5,128,128]{3,2,0,1:T(8,128)S(1)} %get-tuple-element.141), channel_id=1, source_target_pairs={{1,0},{2,1},{3,2},{32,3},{33,32},{34,33},{35,34},{64,35},{65,64},{... | collective-permute-start | bytes 1966088 | tf_op jit(solution)/shard_map/ppermute | solution.py:19
  69.1 13.3 %collective-permute-done = f32[2,5,128,128]{3,2,0,1:T(8,128)S(1)} collective-permute-done((f32[2,5,128,128]{3,2,0,1:T(8,128)S(1)}, f32[2,5,128,128]{3,2,0,1:T(8,128)S(1)}, u32[]{:S(2)}, u32[]{:S(2)}) %collective-permute-start) | collective-permute-done | bytes 655392 | tf_op jit(solution)/shard_map/ppermute | solution.py:17
  82.5 0.0 copy-done
  82.5 0.0 copy-start.1
  82.5 0.6 constant_dynamic-update-slice_fusion.3
  83.1 0.3 copy-done.1
  83.5 1.4 %convolution_bitcast_fusion.9 = f32[8,3,16,128]{3,2,0,1:T(8,128)S(1)} fusion(f32[10,5,128,128]{3,2,0,1:T(8,128)S(1)} %get-tuple-element.144, f32[8,5,16,128]{3,2,0,1:T(8,128)S(1)} %copy-done.1), kind=kOutput, calls=%fused_computation.17 | convolution fusion | flops 75497472 | bytes 3538944 | tf_op jit(solution)/shard_map/iab,itbc->itac/dot_general | solution.py:35
  84.9 1.9 %fusion.7 = f32[8,5,16,128]{3,2,0,1:T(8,128)S(1)} fusion(f32[8,5,16,128]{3,2,0,1:T(8,128)S(1)} %scatter-add.26, f32[10,5,128,128]{3,2,0,1:T(8,128)S(1)} %get-tuple-element.144, f32[8,5,16,128]{3,2,0,1:T(8,128)S(1)} %copy-done.1), kind=kOutput, calls=%fused_computation.13 | convolution fusion | flops 100728832 | bytes 3866624 | tf_op jit(solution)/shard_map/iab,itbc->itac/dot_general | solution.py:35
  86.8 1.7 %fusion.1 = f32[8,5,16,128]{3,2,0,1:T(8,128)S(1)} fusion(f32[8,5,16,128]{3,2,0,1:T(8,128)S(1)} %fusion.7, f32[8,5,128,128]{3,2,0,1:T(8,128)S(1)} %copy-done, f32[8,5,16,128]{3,2,0,1:T(8,128)S(1)} %copy-done.1), kind=kOutput, calls=%fused_computation.3 | convolution fusion | flops 125911040 | bytes 3342336 | tf_op jit(solution)/shard_map/iab,itbc->itac/dot_general | solution.py:35
  88.4 0.0 collective-permute-done.1
  88.5 1.9 %fusion.5 = f32[8,4,16,128]{3,2,0,1:T(8,128)S(1)} fusion(f32[10,5,128,128]{3,2,0,1:T(8,128)S(1)} %constant_dynamic-update-slice_fusion.2, f32[8,5,16,128]{3,2,0,1:T(8,128)S(1)} %fusion.1, f32[8,5,16,128]{3,2,0,1:T(8,128)S(1)} %copy-done.1), kind=kOutput, calls=%fused_computation.10 | convolution fusion | flops 100728832 | bytes 3866624 | tf_op jit(solution)/shard_map/iab,itbc->itac/dot_general | solution.py:35
  90.4 1.4 %fusion.9 = f32[8,5,16,128]{3,2,0,1:T(8,128)S(1)} fusion(f32[8,5,16,128]{3,2,0,1:T(8,128)S(1)} %constant_dynamic-update-slice_fusion.5, f32[8,4,16,128]{3,2,0,1:T(8,128)S(1)} %fusion.5, f32[10,5,128,128]{3,2,0,1:T(8,128)S(1)} %constant_dynamic-update-slice_fusion.2, f32[8,5,16,128]{3,2,0,1:T(8,128)S(1)} %copy-done.1), kind=kOutput, calls=%fused_computation.23 | convolution fusion | flops 75546624 | bytes 3735552 | tf_op jit(solution)/shard_map/iab,itbc->itac/dot_general | solution.py:35
  91.8 0.1 broadcast_multiply_fusion
  92.0 1.4 %convolution_bitcast_fusion.7 = f32[8,3,16,128]{3,2,0,1:T(8,128)S(1)} fusion(f32[10,5,128,128]{3,2,0,1:T(8,128)S(1)} %get-tuple-element.144, f32[8,5,16,128]{3,2,0,1:T(8,128)S(1)} %broadcast_multiply_fusion), kind=kOutput, calls=%fused_computation.15 | convolution fusion | flops 75497472 | bytes 3538944 | tf_op jit(solution)/shard_map/iab,itbc->itac/dot_general | solution.py:35
  93.4 1.9 %fusion.4 = f32[8,5,16,128]{3,2,0,1:T(8,128)S(1)} fusion(f32[8,5,16,128]{3,2,0,1:T(8,128)S(1)} %scatter-add.34, f32[10,5,128,128]{3,2,0,1:T(8,128)S(1)} %get-tuple-element.144, f32[8,5,16,128]{3,2,0,1:T(8,128)S(1)} %broadcast_multiply_fusion), kind=kOutput, calls=%fused_computation.8 | convolution fusion | flops 100728832 | bytes 3866624 | tf_op jit(solution)/shard_map/iab,itbc->itac/dot_general | solution.py:35
  95.3 1.8 %fusion = f32[8,5,16,128]{3,2,0,1:T(8,128)S(1)} fusion(f32[8,5,16,128]{3,2,0,1:T(8,128)S(1)} %fusion.4, f32[8,5,128,128]{3,2,0,1:T(8,128)S(1)} %copy-done, f32[8,5,16,128]{3,2,0,1:T(8,128)S(1)} %broadcast_multiply_fusion), kind=kOutput, calls=%fused_computation.1 | convolution fusion | flops 125911040 | bytes 3342336 | tf_op jit(solution)/shard_map/iab,itbc->itac/dot_general | solution.py:35
  97.1 1.9 %fusion.2 = f32[8,4,16,128]{3,2,0,1:T(8,128)S(1)} fusion(f32[10,5,128,128]{3,2,0,1:T(8,128)S(1)} %constant_dynamic-update-slice_fusion.2, f32[8,5,16,128]{3,2,0,1:T(8,128)S(1)} %fusion, f32[8,5,16,128]{3,2,0,1:T(8,128)S(1)} %broadcast_multiply_fusion), kind=kOutput, calls=%fused_computation.5 | convolution fusion | flops 100728832 | bytes 3866624 | tf_op jit(solution)/shard_map/iab,itbc->itac/dot_general | solution.py:35
  99.0 1.4 %fusion.8 = f32[8,5,16,128]{3,2,0,1:T(8,128)S(1)} fusion(f32[8,5,16,128]{3,2,0,1:T(8,128)S(1)} %constant_dynamic-update-slice_fusion.4, f32[8,4,16,128]{3,2,0,1:T(8,128)S(1)} %fusion.2, f32[10,5,128,128]{3,2,0,1:T(8,128)S(1)} %constant_dynamic-update-slice_fusion.2, f32[8,5,16,128]{3,2,0,1:T(8,128)S(1)} %broadcast_multiply_fusion), kind=kOutput, calls=%fused_computation.21 | convolution fusion | flops 75546624 | bytes 3735552 | tf_op jit(solution)/shard_map/iab,itbc->itac/dot_general | solution.py:35
  100.5 0.1 multiply_subtract_fusion
  100.6 0.7 copy.25
  (6 shorter events, 0.2 us)
Async XLA Ops:
  6.5 50.9 %all-gather.2.cloned.1.call-start = ((), (), s32[]{:S(2)}) async-start(), calls=%async_computation | async-start | bytes 2949120 | tf_op jit(solution)/shard_map/all_gather | solution.py:44
  57.5 25.0 %copy-start = (f32[8,5,128,128]{3,2,0,1:T(8,128)S(1)}, f32[8,5,128,128]{3,2,0,1:T(8,128)}, u32[]{:S(2)}) copy-start(f32[8,5,128,128]{3,2,0,1:T(8,128)} %all-gather.2.cloned.1.call-done) | copy-start | bytes 7864324
  59.0 23.4 %collective-permute-start = (f32[2,5,128,128]{3,2,0,1:T(8,128)S(1)}, f32[2,5,128,128]{3,2,0,1:T(8,128)S(1)}, u32[]{:S(2)}, u32[]{:S(2)}) collective-permute-start(f32[2,5,128,128]{3,2,0,1:T(8,128)S(1)} %get-tuple-element.142), channel_id=1, source_target_pairs={{0,1},{1,2},{2,3},{3,32},{32,33},{33,34},{34,35},{35,64},{64,65},{... | collective-permute-start | bytes 1966088 | tf_op jit(solution)/shard_map/ppermute | solution.py:17
  62.1 26.3 %collective-permute-start.1 = (f32[2,5,128,128]{3,2,0,1:T(8,128)S(1)}, f32[2,5,128,128]{3,2,0,1:T(8,128)S(1)}, u32[]{:S(2)}, u32[]{:S(2)}) collective-permute-start(f32[2,5,128,128]{3,2,0,1:T(8,128)S(1)} %get-tuple-element.141), channel_id=1, source_target_pairs={{1,0},{2,1},{3,2},{32,3},{33,32},{34,33},{35,34},{64,35},{65,64},{... | collective-permute-start | bytes 1966088 | tf_op jit(solution)/shard_map/ppermute | solution.py:19
  82.5 1.0 copy-start.1
Sparse Core Ops, SparseCore 0:
  9.4 47.9 all-gather.1
where the time goes:
time: 108 us
  waiting for transfers between devices  61.7 us (57%)
  matrix products  16.7 us (15%)
  between operations  13.5 us (12%)
  starting transfers between devices  10 us (9%)
  local copies, waits for them, and re-layouts  3.51 us (3%)
  other arithmetic  2.73 us (3%)
    all_gather x1, waiting for transfers between devices, shards(): whole_tiles = lax.all_gather(masked, 'col', axis=2, tiled=True)  48.3 us
    dot_general x10, matrix products, banded_local(): jnp.einsum('iab,itbc->itac', left_tiles[:, source], partner, precision=la...  16.7 us
    ppermute x1, waiting for transfers between devices, with_halo(): lax.ppermute(tail, axis, [(i, (i + 1) % count) for i in range(count)])  13.3 us
    ppermute x1, starting transfers between devices, with_halo(): lax.ppermute(head, axis, [((i + 1) % count, i) for i in range(count)])  6.94 us
    ppermute x1, starting transfers between devices, with_halo(): lax.ppermute(tail, axis, [(i, (i + 1) % count) for i in range(count)])  3.1 us
  transfers between devices with their start and end apart: 3, of which 2 were waited for; matrix products, arithmetic and copies ran while one was open for 5% of the time, Pallas kernels for 0%

commit v1 on v0

--- a/solution.py
+++ b/solution.py
@@ -5,6 +5,29 @@
 
 HALF = 2
 WIDE = 5
+
+
+def convert_packet(panel, axis_tag):
+    latest = jax.lax.axis_size(axis_tag)
+    y_new = jax.lax.axis_index(axis_tag)
+    plain, current_block, part_next = (latest, y_new, panel.shape[2])
+    all_blocks = tuple(((kk, (kk + 1) % plain) for kk in range(plain)))
+    bank = tuple(((kk, (kk - 1) % plain) for kk in range(plain)))
+    p_next = jnp.zeros((*panel.shape[:2], plain * part_next, *panel.shape[3:]), panel.dtype)
+    p_next = lax.dynamic_update_slice_in_dim(p_next, panel, current_block * part_next, axis=2)
+    local_out = back = panel
+    side_arr = plain // 2
+    for i0 in range(1, side_arr + 1):
+        local_out = jax.lax.ppermute(local_out, axis_name=axis_tag, perm=all_blocks)
+        p_next = lax.dynamic_update_slice_in_dim(
+            p_next, local_out, (current_block - i0) % plain * part_next, axis=2
+        )
+        if i0 < plain - side_arr:
+            back = jax.lax.ppermute(back, perm=bank, axis_name=axis_tag)
+            p_next = lax.dynamic_update_slice_in_dim(
+                p_next, back, (current_block + i0) % plain * part_next, axis=2
+            )
+    return p_next
 
 
 def with_halo(cells, sides, width):
@@ -41,7 +64,7 @@
 
 def shards(density, pattern):
     masked = density * pattern[:, :, None, None].astype(jnp.float32)
-    whole_tiles = lax.all_gather(masked, "col", axis=2, tiled=True)
+    whole_tiles = convert_packet(masked, "col")
     extended = with_halo(whole_tiles, ((("row", "depth"), 0),), HALF)
     square = banded_local(masked, extended, pattern)
     cube = banded_local(square, extended, pattern)

time: 108 us -> 91.6 us (0.85)
  starting transfers between devices: 10 us -> 38.7 us
  waiting for transfers between devices: 61.7 us -> 34.5 us
  between operations: 13.5 us -> 0.39 us
  matrix products: 16.7 us -> 12.5 us
  local copies, waits for them, and re-layouts: 3.51 us -> 1.55 us
    all_gather x1 -> x0, waiting for transfers between devices: 48.3 us -> none  [shards(): whole_tiles = lax.all_gather(masked, 'col', axis=2, tiled=True)]
    ppermute x0 -> x7, starting transfers between devices: none -> 28.3 us  [the longest x3 17.7 us: convert_packet(): back = jax.lax.ppermute(back, perm=bank, axis_name=axis_tag)]
    ppermute x0 -> x7, waiting for transfers between devices: none -> 20 us  [the longest x4 20 us: convert_packet(): local_out = jax.lax.ppermute(local_out, axis_name=axis_tag, perm=all_blocks)]
    dot_general x10, matrix products: 16.7 us -> 12.5 us  [banded_local(): jnp.einsum('iab,itbc->itac', left_tiles[:, source], partner, precision=la...]
    slice x1, local copies, waits for them, and re-layouts: 1.53 us -> 0.13 us  [with_halo(): head = lax.slice_in_dim(cells, 0, width, axis=dim)]
    ppermute x1, waiting for transfers between devices: 0.01 us -> 1.18 us  [with_halo(): lax.ppermute(head, axis, [((i + 1) % count, i) for i in range(count)])]
  transfers between devices with their start and end apart: 3 -> 9, of which waited for: 2 -> 6; matrix products, arithmetic and copies ran while one was open for 5% -> 1% of each run, Pallas kernels for 0% -> 0%
where the time goes in v1:
time: 91.6 us; the launch traced here: 90.7 us
  starting transfers between devices  38.7 us (42%)
  waiting for transfers between devices  34.5 us (38%)
  matrix products  12.5 us (14%)
  other arithmetic  3.08 us (3%)
  local copies, waits for them, and re-layouts  1.55 us (2%)
    ppermute x4, waiting for transfers between devices, convert_packet(): local_out = jax.lax.ppermute(local_out, axis_name=axis_tag, perm=all_blocks)  20 us
    ppermute x3, starting transfers between devices, convert_packet(): back = jax.lax.ppermute(back, perm=bank, axis_name=axis_tag)  17.7 us
    ppermute x1, waiting for transfers between devices, with_halo(): lax.ppermute(tail, axis, [(i, (i + 1) % count) for i in range(count)])  13.3 us
    dot_general x10, matrix products, banded_local(): jnp.einsum('iab,itbc->itac', left_tiles[:, source], partner, precision=la...  12.5 us
    ppermute x4, starting transfers between devices, convert_packet(): local_out = jax.lax.ppermute(local_out, axis_name=axis_tag, perm=all_blocks)  10.6 us
    ppermute x1, starting transfers between devices, with_halo(): lax.ppermute(head, axis, [((i + 1) % count, i) for i in range(count)])  7.29 us
    ppermute x1, starting transfers between devices, with_halo(): lax.ppermute(tail, axis, [(i, (i + 1) % count) for i in range(count)])  3.12 us
  transfers between devices with their start and end apart: 9, of which 6 were waited for; matrix products, arithmetic and copies ran while one was open for 1% of the time, Pallas kernels for 0%

profile of v1, /device:TPU:1, one launch (start us, length us, event | category | flops | bytes accessed | tf_op | source)
XLA Modules:
  0.0 90.7 jit_solution(5755533475365448967)
XLA Ops:
  0.0 0.0 copy-start
  0.0 0.7 convert_element_type.6
  0.7 0.1 copy.3
  0.8 1.1 %copy_multiply_fusion = f32[8,5,16,128]{3,2,0,1:T(8,128)S(1)} fusion(f32[8,5,16,128]{3,2,1,0:T(8,128)} %param.26, f32[8,5]{0,1:T(8,128)S(1)} %copy.3), kind=kLoop, calls=%fused_computation.46 | loop fusion | flops 81920 | bytes 655520 | tf_op jit(solution)/shard_map/mul | solution.py:66
  1.9 4.8 %collective-permute-start = (f32[8,5,16,128]{3,2,0,1:T(8,128)S(1)}, f32[8,5,16,128]{3,2,0,1:T(8,128)S(1)}, u32[]{:S(2)}, u32[]{:S(2)}) collective-permute-start(f32[8,5,16,128]{3,2,0,1:T(8,128)S(1)} %copy_multiply_fusion), channel_id=1, source_target_pairs={{0,4},{4,8},{8,12},{12,16},{16,20},{20,24},{24,28},{28,0},{1,5},{5... | collective-permute-start | bytes 983048 | tf_op jit(solution)/shard_map/ppermute | solution.py:21
  6.7 8.6 %collective-permute-start.1 = (f32[8,5,16,128]{3,2,0,1:T(8,128)S(1)}, f32[8,5,16,128]{3,2,0,1:T(8,128)S(1)}, u32[]{:S(2)}, u32[]{:S(2)}) collective-permute-start(f32[8,5,16,128]{3,2,0,1:T(8,128)S(1)} %copy_multiply_fusion), channel_id=1, source_target_pairs={{0,28},{4,0},{8,4},{12,8},{16,12},{20,16},{24,20},{28,24},{1,29},{... | collective-permute-start | bytes 983048 | tf_op jit(solution)/shard_map/ppermute | solution.py:26
  15.5 0.3 broadcast_in_dim.2
  15.8 0.0 copy-done
  15.8 0.1 copy_dynamic-update-slice_fusion.7
  15.9 4.9 %collective-permute-done = f32[8,5,16,128]{3,2,0,1:T(8,128)S(1)} collective-permute-done((f32[8,5,16,128]{3,2,0,1:T(8,128)S(1)}, f32[8,5,16,128]{3,2,0,1:T(8,128)S(1)}, u32[]{:S(2)}, u32[]{:S(2)}) %collective-permute-start) | collective-permute-done | bytes 327712 | tf_op jit(solution)/shard_map/ppermute | solution.py:21
  20.8 1.9 %collective-permute-start.2 = (f32[8,5,16,128]{3,2,0,1:T(8,128)S(1)}, f32[8,5,16,128]{3,2,0,1:T(8,128)S(1)}, u32[]{:S(2)}, u32[]{:S(2)}) collective-permute-start(f32[8,5,16,128]{3,2,0,1:T(8,128)S(1)} %collective-permute-done), channel_id=1, source_target_pairs={{0,4},{4,8},{8,12},{12,16},{16,20},{20,24},{24,28},{28,0},{1,5},{5... | collective-permute-start | bytes 983048 | tf_op jit(solution)/shard_map/ppermute | solution.py:21
  22.7 0.0 collective-permute-done.1
  22.8 4.6 %collective-permute-start.3 = (f32[8,5,16,128]{3,2,0,1:T(8,128)S(1)}, f32[8,5,16,128]{3,2,0,1:T(8,128)S(1)}, u32[]{:S(2)}, u32[]{:S(2)}) collective-permute-start(f32[8,5,16,128]{3,2,0,1:T(8,128)S(1)} %collective-permute-done.1), channel_id=1, source_target_pairs={{0,28},{4,0},{8,4},{12,8},{16,12},{20,16},{24,20},{28,24},{1,29},{... | collective-permute-start | bytes 983048 | tf_op jit(solution)/shard_map/ppermute | solution.py:26
  27.4 4.5 %collective-permute-done.2 = f32[8,5,16,128]{3,2,0,1:T(8,128)S(1)} collective-permute-done((f32[8,5,16,128]{3,2,0,1:T(8,128)S(1)}, f32[8,5,16,128]{3,2,0,1:T(8,128)S(1)}, u32[]{:S(2)}, u32[]{:S(2)}) %collective-permute-start.2) | collective-permute-done | bytes 327712 | tf_op jit(solution)/shard_map/ppermute | solution.py:21
  31.9 1.9 %collective-permute-start.4 = (f32[8,5,16,128]{3,2,0,1:T(8,128)S(1)}, f32[8,5,16,128]{3,2,0,1:T(8,128)S(1)}, u32[]{:S(2)}, u32[]{:S(2)}) collective-permute-start(f32[8,5,16,128]{3,2,0,1:T(8,128)S(1)} %collective-permute-done.2), channel_id=1, source_target_pairs={{0,4},{4,8},{8,12},{12,16},{16,20},{20,24},{24,28},{28,0},{1,5},{5... | collective-permute-start | bytes 983048 | tf_op jit(solution)/shard_map/ppermute | solution.py:21
  33.8 0.0 collective-permute-done.3
  33.8 4.6 %collective-permute-start.5 = (f32[8,5,16,128]{3,2,0,1:T(8,128)S(1)}, f32[8,5,16,128]{3,2,0,1:T(8,128)S(1)}, u32[]{:S(2)}, u32[]{:S(2)}) collective-permute-start(f32[8,5,16,128]{3,2,0,1:T(8,128)S(1)} %collective-permute-done.3), channel_id=1, source_target_pairs={{0,28},{4,0},{8,4},{12,8},{16,12},{20,16},{24,20},{28,24},{1,29},{... | collective-permute-start | bytes 983048 | tf_op jit(solution)/shard_map/ppermute | solution.py:26
  38.5 3.5 %collective-permute-done.4 = f32[8,5,16,128]{3,2,0,1:T(8,128)S(1)} collective-permute-done((f32[8,5,16,128]{3,2,0,1:T(8,128)S(1)}, f32[8,5,16,128]{3,2,0,1:T(8,128)S(1)}, u32[]{:S(2)}, u32[]{:S(2)}) %collective-permute-start.4) | collective-permute-done | bytes 327712 | tf_op jit(solution)/shard_map/ppermute | solution.py:21
  42.0 1.9 %collective-permute-start.6 = (f32[8,5,16,128]{3,2,0,1:T(8,128)S(1)}, f32[8,5,16,128]{3,2,0,1:T(8,128)S(1)}, u32[]{:S(2)}, u32[]{:S(2)}) collective-permute-start(f32[8,5,16,128]{3,2,0,1:T(8,128)S(1)} %collective-permute-done.4), channel_id=1, source_target_pairs={{0,4},{4,8},{8,12},{12,16},{16,20},{20,24},{24,28},{28,0},{1,5},{5... | collective-permute-start | bytes 983048 | tf_op jit(solution)/shard_map/ppermute | solution.py:21
  44.0 0.0 collective-permute-done.5
  44.1 7.0 %collective-permute-done.6 = f32[8,5,16,128]{3,2,0,1:T(8,128)S(1)} collective-permute-done((f32[8,5,16,128]{3,2,0,1:T(8,128)S(1)}, f32[8,5,16,128]{3,2,0,1:T(8,128)S(1)}, u32[]{:S(2)}, u32[]{:S(2)}) %collective-permute-start.6) | collective-permute-done | bytes 327712 | tf_op jit(solution)/shard_map/ppermute | solution.py:21
  51.1 0.1 fusion.71
  51.2 3.1 %collective-permute-start.7 = (f32[2,5,128,128]{3,2,1,0:T(8,128)S(1)}, f32[2,5,128,128]{3,2,1,0:T(8,128)S(1)}, u32[]{:S(2)}, u32[]{:S(2)}) collective-permute-start(f32[2,5,128,128]{3,2,1,0:T(8,128)S(1)} %get-tuple-element.146), channel_id=1, source_target_pairs={{0,1},{1,2},{2,3},{3,32},{32,33},{33,34},{34,35},{35,64},{64,65},{... | collective-permute-start | bytes 1966088 | tf_op jit(solution)/shard_map/ppermute | solution.py:40
  54.4 7.3 %collective-permute-start.8 = (f32[2,5,128,128]{3,2,1,0:T(8,128)S(1)}, f32[2,5,128,128]{3,2,1,0:T(8,128)S(1)}, u32[]{:S(2)}, u32[]{:S(2)}) collective-permute-start(f32[2,5,128,128]{3,2,1,0:T(8,128)S(1)} %get-tuple-element.145), channel_id=1, source_target_pairs={{1,0},{2,1},{3,2},{32,3},{33,32},{34,33},{35,34},{64,35},{65,64},{... | collective-permute-start | bytes 1966088 | tf_op jit(solution)/shard_map/ppermute | solution.py:42
  61.7 13.3 %collective-permute-done.7 = f32[2,5,128,128]{3,2,1,0:T(8,128)S(1)} collective-permute-done((f32[2,5,128,128]{3,2,1,0:T(8,128)S(1)}, f32[2,5,128,128]{3,2,1,0:T(8,128)S(1)}, u32[]{:S(2)}, u32[]{:S(2)}) %collective-permute-start.7) | collective-permute-done | bytes 655392 | tf_op jit(solution)/shard_map/ppermute | solution.py:40
  75.0 1.2 %collective-permute-done.8 = f32[2,5,128,128]{3,2,1,0:T(8,128)S(1)} collective-permute-done((f32[2,5,128,128]{3,2,1,0:T(8,128)S(1)}, f32[2,5,128,128]{3,2,1,0:T(8,128)S(1)}, u32[]{:S(2)}, u32[]{:S(2)}) %collective-permute-start.8) | collective-permute-done | bytes 655392 | tf_op jit(solution)/shard_map/ppermute | solution.py:42
  76.2 0.4 pad_maximum_fusion.1
  76.6 1.1 %fusion.45 = f32[8,3,16,128]{3,2,0,1:T(8,128)S(1)} fusion(f32[8,3,128,128]{3,2,1,0:T(8,128)S(1)} %get-tuple-element.142, f32[8,5,16,128]{3,2,0,1:T(8,128)S(1)} %copy_multiply_fusion), kind=kOutput, calls=%fused_computation.34 | convolution fusion | flops 75497472 | bytes 1835008 | tf_op jit(solution)/shard_map/iab,itbc->itac/dot_general | solution.py:58
  77.8 0.5 fusion.4
  78.3 1.2 %add_dynamic-update-slice_fusion.1 = f32[8,5,16,128]{3,2,0,1:T(8,128)S(1)} fusion(f32[8,5,16,128]{3,2,0,1:T(8,128)S(1)} %scatter-add.26, f32[8,5,16,128]{3,2,0,1:T(8,128)S(1)} %copy_multiply_fusion, f32[8,4,128,128]{3,2,1,0:T(8,128)S(1)} %get-tuple-element.144), kind=kOutput, calls=%fused_computation.51 | convolution fusion | flops 100728832 | bytes 2686976 | tf_op jit(solution)/shard_map/iab,itbc->itac/dot_general | solution.py:58
  79.5 1.7 %fusion.24 = f32[8,5,16,128]{3,2,0,1:T(8,128)S(1)} fusion(f32[8,5,16,128]{3,2,0,1:T(8,128)S(1)} %add_dynamic-update-slice_fusion.1, f32[8,5,128,128]{3,2,1,0:T(8,128)S(1)} %copy_dynamic-update-slice_fusion, f32[8,5,16,128]{3,2,0,1:T(8,128)S(1)} %copy_multiply_fusion), kind=kOutput, calls=%fused_computation.27 | convolution fusion | flops 125911040 | bytes 3342336 | tf_op jit(solution)/shard_map/iab,itbc->itac/dot_general | solution.py:58
  81.1 1.2 %constant_dynamic-update-slice_fusion.1 = (f32[8,5,16,128]{3,2,0,1:T(8,128)S(1)}, f32[8,4,16,128]{3,2,0,1:T(8,128)S(1)}) fusion(f32[8,5,16,128]{3,2,0,1:T(8,128)S(1)} %fusion.24, f32[8,5,16,128]{3,2,0,1:T(8,128)S(1)} %copy_multiply_fusion, f32[8,4,128,128]{3,2,1,0:T(8,128)S(1)} %get-tuple-element.143), kind=kOutput, calls=%fused_computation.68 | convolution fusion | flops 100728832 | bytes 2949120 | tf_op jit(solution)/shard_map/iab,itbc->itac/dot_general | solution.py:58
  82.3 1.1 %fusion.58 = f32[8,5,16,128]{3,2,0,1:T(8,128)S(1)} fusion(f32[8,5,16,128]{3,2,0,1:T(8,128)S(1)} %get-tuple-element.147, f32[8,4,16,128]{3,2,0,1:T(8,128)S(1)} %get-tuple-element.148, f32[8,5,16,128]{3,2,0,1:T(8,128)S(1)} %copy_multiply_fusion, f32[8,3,128,128]{3,2,1,0:T(8,128)S(1)} %get-tuple-element.141), kind=kOutput, calls=%fused_computation.55 | convolution fusion | flops 75546624 | bytes 2031616 | tf_op jit(solution)/shard_map/iab,itbc->itac/dot_general | solution.py:58
  83.4 0.1 broadcast_multiply_fusion
  83.6 1.1 %fusion.48 = f32[8,3,16,128]{3,2,0,1:T(8,128)S(1)} fusion(f32[8,3,128,128]{3,2,1,0:T(8,128)S(1)} %get-tuple-element.142, f32[8,5,16,128]{3,2,0,1:T(8,128)S(1)} %broadcast_multiply_fusion), kind=kOutput, calls=%fused_computation.35 | convolution fusion | flops 75497472 | bytes 1835008 | tf_op jit(solution)/shard_map/iab,itbc->itac/dot_general | solution.py:58
  84.7 1.2 %add_dynamic-update-slice_fusion = f32[8,5,16,128]{3,2,0,1:T(8,128)S(1)} fusion(f32[8,5,16,128]{3,2,0,1:T(8,128)S(1)} %scatter-add.34, f32[8,5,16,128]{3,2,0,1:T(8,128)S(1)} %broadcast_multiply_fusion, f32[8,4,128,128]{3,2,1,0:T(8,128)S(1)} %get-tuple-element.144), kind=kOutput, calls=%fused_computation.50 | convolution fusion | flops 100728832 | bytes 2686976 | tf_op jit(solution)/shard_map/iab,itbc->itac/dot_general | solution.py:58
  85.9 1.7 %fusion.30 = f32[8,5,16,128]{3,2,0,1:T(8,128)S(1)} fusion(f32[8,5,16,128]{3,2,0,1:T(8,128)S(1)} %add_dynamic-update-slice_fusion, f32[8,5,128,128]{3,2,1,0:T(8,128)S(1)} %copy_dynamic-update-slice_fusion, f32[8,5,16,128]{3,2,0,1:T(8,128)S(1)} %broadcast_multiply_fusion), kind=kOutput, calls=%fused_computation.29 | convolution fusion | flops 125911040 | bytes 3342336 | tf_op jit(solution)/shard_map/iab,itbc->itac/dot_general | solution.py:58
  87.6 1.2 %constant_dynamic-update-slice_fusion = (f32[8,5,16,128]{3,2,0,1:T(8,128)S(1)}, f32[8,4,16,128]{3,2,0,1:T(8,128)S(1)}) fusion(f32[8,5,16,128]{3,2,0,1:T(8,128)S(1)} %fusion.30, f32[8,5,16,128]{3,2,0,1:T(8,128)S(1)} %broadcast_multiply_fusion, f32[8,4,128,128]{3,2,1,0:T(8,128)S(1)} %get-tuple-element.143), kind=kOutput, calls=%fused_computation.67 | convolution fusion | flops 100728832 | bytes 2949120 | tf_op jit(solution)/shard_map/iab,itbc->itac/dot_general | solution.py:58
  88.8 1.1 %fusion.57 = f32[8,5,16,128]{3,2,0,1:T(8,128)S(1)} fusion(f32[8,5,16,128]{3,2,0,1:T(8,128)S(1)} %get-tuple-element.149, f32[8,4,16,128]{3,2,0,1:T(8,128)S(1)} %get-tuple-element.150, f32[8,5,16,128]{3,2,0,1:T(8,128)S(1)} %broadcast_multiply_fusion, f32[8,3,128,128]{3,2,1,0:T(8,128)S(1)} %get-tuple-element.141), kind=kOutput, calls=%fused_computation.53 | convolution fusion | flops 75546624 | bytes 2031616 | tf_op jit(solution)/shard_map/iab,itbc->itac/dot_general | solution.py:58
  89.9 0.1 multiply_subtract_fusion
  90.0 0.7 copy.23
  (9 shorter events, 0.3 us)
Async XLA Ops:
  0.0 15.8 %copy-start = (f32[8,5,16,128]{3,2,1,0:T(8,128)S(1)}, f32[8,5,16,128]{3,2,1,0:T(8,128)}, u32[]{:S(2)}) copy-start(f32[8,5,16,128]{3,2,1,0:T(8,128)} %param.26) | copy-start | bytes 983044
  1.9 18.9 %collective-permute-start = (f32[8,5,16,128]{3,2,0,1:T(8,128)S(1)}, f32[8,5,16,128]{3,2,0,1:T(8,128)S(1)}, u32[]{:S(2)}, u32[]{:S(2)}) collective-permute-start(f32[8,5,16,128]{3,2,0,1:T(8,128)S(1)} %copy_multiply_fusion), channel_id=1, source_target_pairs={{0,4},{4,8},{8,12},{12,16},{16,20},{20,24},{24,28},{28,0},{1,5},{5... | collective-permute-start | bytes 983048 | tf_op jit(solution)/shard_map/ppermute | solution.py:21
  6.7 16.0 %collective-permute-start.1 = (f32[8,5,16,128]{3,2,0,1:T(8,128)S(1)}, f32[8,5,16,128]{3,2,0,1:T(8,128)S(1)}, u32[]{:S(2)}, u32[]{:S(2)}) collective-permute-start(f32[8,5,16,128]{3,2,0,1:T(8,128)S(1)} %copy_multiply_fusion), channel_id=1, source_target_pairs={{0,28},{4,0},{8,4},{12,8},{16,12},{20,16},{24,20},{28,24},{1,29},{... | collective-permute-start | bytes 983048 | tf_op jit(solution)/shard_map/ppermute | solution.py:26
  20.8 11.1 %collective-permute-start.2 = (f32[8,5,16,128]{3,2,0,1:T(8,128)S(1)}, f32[8,5,16,128]{3,2,0,1:T(8,128)S(1)}, u32[]{:S(2)}, u32[]{:S(2)}) collective-permute-start(f32[8,5,16,128]{3,2,0,1:T(8,128)S(1)} %collective-permute-done), channel_id=1, source_target_pairs={{0,4},{4,8},{8,12},{12,16},{16,20},{20,24},{24,28},{28,0},{1,5},{5... | collective-permute-start | bytes 983048 | tf_op jit(solution)/shard_map/ppermute | solution.py:21
  22.8 11.1 %collective-permute-start.3 = (f32[8,5,16,128]{3,2,0,1:T(8,128)S(1)}, f32[8,5,16,128]{3,2,0,1:T(8,128)S(1)}, u32[]{:S(2)}, u32[]{:S(2)}) collective-permute-start(f32[8,5,16,128]{3,2,0,1:T(8,128)S(1)} %collective-permute-done.1), channel_id=1, source_target_pairs={{0,28},{4,0},{8,4},{12,8},{16,12},{20,16},{24,20},{28,24},{1,29},{... | collective-permute-start | bytes 983048 | tf_op jit(solution)/shard_map/ppermute | solution.py:26
  31.9 10.1 %collective-permute-start.4 = (f32[8,5,16,128]{3,2,0,1:T(8,128)S(1)}, f32[8,5,16,128]{3,2,0,1:T(8,128)S(1)}, u32[]{:S(2)}, u32[]{:S(2)}) collective-permute-start(f32[8,5,16,128]{3,2,0,1:T(8,128)S(1)} %collective-permute-done.2), channel_id=1, source_target_pairs={{0,4},{4,8},{8,12},{12,16},{16,20},{20,24},{24,28},{28,0},{1,5},{5... | collective-permute-start | bytes 983048 | tf_op jit(solution)/shard_map/ppermute | solution.py:21
  33.8 10.2 %collective-permute-start.5 = (f32[8,5,16,128]{3,2,0,1:T(8,128)S(1)}, f32[8,5,16,128]{3,2,0,1:T(8,128)S(1)}, u32[]{:S(2)}, u32[]{:S(2)}) collective-permute-start(f32[8,5,16,128]{3,2,0,1:T(8,128)S(1)} %collective-permute-done.3), channel_id=1, source_target_pairs={{0,28},{4,0},{8,4},{12,8},{16,12},{20,16},{24,20},{28,24},{1,29},{... | collective-permute-start | bytes 983048 | tf_op jit(solution)/shard_map/ppermute | solution.py:26
  42.0 9.0 %collective-permute-start.6 = (f32[8,5,16,128]{3,2,0,1:T(8,128)S(1)}, f32[8,5,16,128]{3,2,0,1:T(8,128)S(1)}, u32[]{:S(2)}, u32[]{:S(2)}) collective-permute-start(f32[8,5,16,128]{3,2,0,1:T(8,128)S(1)} %collective-permute-done.4), channel_id=1, source_target_pairs={{0,4},{4,8},{8,12},{12,16},{16,20},{20,24},{24,28},{28,0},{1,5},{5... | collective-permute-start | bytes 983048 | tf_op jit(solution)/shard_map/ppermute | solution.py:21
  51.2 23.8 %collective-permute-start.7 = (f32[2,5,128,128]{3,2,1,0:T(8,128)S(1)}, f32[2,5,128,128]{3,2,1,0:T(8,128)S(1)}, u32[]{:S(2)}, u32[]{:S(2)}) collective-permute-start(f32[2,5,128,128]{3,2,1,0:T(8,128)S(1)} %get-tuple-element.146), channel_id=1, source_target_pairs={{0,1},{1,2},{2,3},{3,32},{32,33},{33,34},{34,35},{35,64},{64,65},{... | collective-permute-start | bytes 1966088 | tf_op jit(solution)/shard_map/ppermute | solution.py:40
  54.4 21.8 %collective-permute-start.8 = (f32[2,5,128,128]{3,2,1,0:T(8,128)S(1)}, f32[2,5,128,128]{3,2,1,0:T(8,128)S(1)}, u32[]{:S(2)}, u32[]{:S(2)}) collective-permute-start(f32[2,5,128,128]{3,2,1,0:T(8,128)S(1)} %get-tuple-element.145), channel_id=1, source_target_pairs={{1,0},{2,1},{3,2},{32,3},{33,32},{34,33},{35,34},{64,35},{65,64},{... | collective-permute-start | bytes 1966088 | tf_op jit(solution)/shard_map/ppermute | solution.py:42
